TPU v7x, 32 devices: a whole 2x2x4 slice. The times are simulated.
32 devices in a mesh: gx: 8 (over z, y), gy: 4 (over x, core).
Axes of the slice: x: 2, y: 2, z: 4, core: 2. Of those that a mesh axis runs over, the one named last changes fastest.
Arguments:
- template: bfloat16 [256, 128, 256], P('gx', 'gy'), may hold values from -6 to 6
- target_image: bfloat16 [256, 128, 256], P('gx', 'gy'), may hold values from -6 to 6
- velocity: float32 [3, 256, 128, 256], P(None, 'gx', 'gy'), may hold values from -6 to 6
- operators: bfloat16 [64, 3, 32, 32], replicated, may hold values from -1 to 1
- route: int32 [2, 8, 4, 8, 1], P(None, 'gx', 'gy'), may hold values from 0 to 7; in each aligned block of 8 rows (0 to 7, 8 to 15, ..., all dimensions but the last counted through in order) at most 2 rows name the same one
- target_brick: int32 [2, 8, 4, 8], P(None, 'gx', 'gy'), may hold values from 0 to 7
- operator_index: int32 [2, 8, 4, 8], P(None, 'gx', 'gy'), may hold values from 0 to 63
Outputs:
- velocity_grad: float32 [3, 256, 128, 256], P(None, 'gx', 'gy')
- template_grad: bfloat16 [256, 128, 256], P('gx', 'gy')
Inputs may be any that keep to these rules, and one draw needn't show every extreme that they name: `route`: in every step, no device sends more than 2 of its bricks to one destination device, and some device sends exactly 2 to one; the destination keeps the second index.
All inputs are finite; a program needn't handle non-finite values.
Results may differ from a plain program's by a relative error of at most 0.0085.
Values may be sent and summed in bfloat16 or wider, within the bound.
No kernel may reach another device: no remote copies, remote signals or barrier semaphores. Data moves between devices by JAX's collectives and lax.ppermute only.
A program may use at most 128 MiB of HBM per device.

v0:
```python
import jax
import jax.numpy as jnp
from jax import lax
from jax.sharding import PartitionSpec as P

STEPS = 2


HIGHEST_PRECISION = lax.Precision.HIGHEST


def extended(value, sides, width):
    for axis, dim in sides:
        size, length = (lax.axis_size(axis), value.shape[dim])
        up = [(i, (i + 1) % size) for i in range(size - 1)]
        down = [(j, i) for i, j in up]
        last = lax.slice_in_dim(value, length - width, length, axis=dim)
        initial = lax.slice_in_dim(value, 0, width, axis=dim)
        before = lax.ppermute(last, axis, up)
        after = lax.ppermute(initial, axis, down)
        value = jnp.concatenate([before, value, after], axis=dim)
    return value


def sixth_order(padded, axis_id):
    array_rank = padded.ndim

    def shifted(offset):
        slicer = []
        for dimension in range(array_rank):
            if dimension == array_rank - 3 + axis_id:
                slicer.append(slice(3 + offset, padded.shape[dimension] - 3 + offset))
            else:
                slicer.append(slice(3, padded.shape[dimension] - 3))
        return padded[tuple(slicer)]

    return (
        0.75 * (shifted(1) - shifted(-1))
        - 0.15 * (shifted(2) - shifted(-2))
        + (shifted(3) - shifted(-3)) / 60.0
    )


def pad_depth(field_in):
    widths = [(0, 0)] * (field_in.ndim - 1) + [(3, 3)]
    return jnp.pad(field_in, widths)


def split_bricks(field_in, edge_cells):
    cells_x, cells_y, depth_cells = field_in.shape
    brick_total = depth_cells // edge_cells
    shaped = field_in.reshape(cells_x, cells_y, brick_total, edge_cells).transpose(2, 0, 1, 3)
    return shaped.reshape(brick_total, cells_x, cells_y * edge_cells)


def join_bricks(bricks, edge_cells):
    brick_total = bricks.shape[0]
    shaped = bricks.reshape(brick_total, edge_cells, edge_cells, edge_cells).transpose(1, 2, 0, 3)
    return shaped.reshape(edge_cells, edge_cells, brick_total * edge_cells)


def lookup(operators, indices):
    tables = operators.shape[0]
    one_hot = (indices[:, None] == jnp.arange(tables, dtype=jnp.int32)[None, :]).astype(
        jnp.bfloat16
    )
    chosen = jnp.dot(one_hot, operators.reshape(tables, -1), preferred_element_type=jnp.float32)
    return chosen.astype(jnp.bfloat16).reshape((indices.shape[0],) + operators.shape[1:])


def apply_operator(matrices, bricks, flipped):
    brick_total, edge_cells = (bricks.shape[0], bricks.shape[1])
    square = edge_cells * edge_cells
    if flipped:
        forms_list = ["mar,max->mrx", "mbr,mby->mry", "mcr,mcz->mrz"]
    else:
        forms_list = ["mar,mxa->mrx", "mbr,myb->mry", "mcr,mzc->mrz"]
    section_one = jnp.einsum(
        forms_list[0], bricks, matrices[:, 0], preferred_element_type=jnp.float32
    )
    view_one = section_one.reshape(brick_total, edge_cells, square)
    section_two = jnp.einsum(
        forms_list[1], view_one, matrices[:, 1].astype(jnp.float32), precision=HIGHEST_PRECISION
    )
    view_two = section_two.reshape(brick_total, edge_cells, square)
    section_three = jnp.einsum(
        forms_list[2], view_two, matrices[:, 2].astype(jnp.float32), precision=HIGHEST_PRECISION
    )
    return section_three.reshape(brick_total, edge_cells, square)


def shards(template, target_image, velocity, operators, route, target_brick, operator_index):
    edge_cells = operators.shape[2]
    brick_total = template.shape[2] // edge_cells
    peer_count = lax.axis_size("gx")
    capacity = max(2, 2 * brick_total // peer_count)
    slot_count = peer_count * capacity
    volume = edge_cells * edge_cells * edge_cells
    brick_ids = jnp.arange(brick_total, dtype=jnp.int32)
    slot_ids = jnp.arange(slot_count, dtype=jnp.int32)
    states = [template]
    arrivals = []
    sendlists = []
    for section_id in range(STEPS):
        destination = route[section_id, 0, 0, :, 0]
        landing = target_brick[section_id, 0, 0]
        chosen_ops = operator_index[section_id, 0, 0]
        earlier = (destination[:, None] == destination[None, :]) & (
            brick_ids[:, None] > brick_ids[None, :]
        )
        position = destination * capacity + jnp.sum(earlier.astype(jnp.int32), axis=1)
        placing = slot_ids[:, None] == position[None, :]
        place_int = placing.astype(jnp.int32)
        place_half = placing.astype(jnp.bfloat16)
        slot_landing = (jnp.sum(place_int * (landing + 1)[None, :], axis=1) - 1).reshape(
            peer_count, capacity
        )
        bricks = split_bricks(states[-1], edge_cells)
        slot_ops = (jnp.sum(place_int * (chosen_ops + 1)[None, :], axis=1) - 1).reshape(
            peer_count, capacity
        )
        packed = jnp.dot(
            place_half, bricks.reshape(brick_total, volume), preferred_element_type=jnp.float32
        ).astype(jnp.bfloat16)
        received, got_landing, got_ops = (
            lax.all_to_all(
                packed.reshape(peer_count, capacity, volume),
                "gx",
                split_axis=0,
                concat_axis=0,
                tiled=True,
            ),
            lax.all_to_all(slot_landing, "gx", split_axis=0, concat_axis=0, tiled=True),
            lax.all_to_all(slot_ops, "gx", split_axis=0, concat_axis=0, tiled=True),
        )
        flat_ops = got_ops.reshape(slot_count)
        incoming = apply_operator(
            lookup(operators, flat_ops),
            received.reshape(slot_count, edge_cells, edge_cells * edge_cells),
            False,
        )
        incoming = incoming.astype(jnp.bfloat16).reshape(slot_count, volume)
        arrivals.append((got_landing.reshape(slot_count), flat_ops))
        sendlists.append((place_half, chosen_ops))
        gather_rows = (brick_ids[:, None] == got_landing.reshape(slot_count)[None, :]).astype(
            jnp.bfloat16
        )
        summed = jnp.dot(gather_rows, incoming, preferred_element_type=jnp.float32).astype(
            jnp.bfloat16
        )
        states.append(
            join_bricks(
                summed.reshape(brick_total, edge_cells, edge_cells * edge_cells), edge_cells
            )
        )
    adjoint = (states[-1].astype(jnp.float32) - target_image.astype(jnp.float32)).astype(
        jnp.bfloat16
    )
    accumulated = jnp.zeros((3,) + template.shape, jnp.float32)
    for section_id in reversed(range(STEPS)):
        rimmed = extended(states[section_id], (("gx", 0), ("gy", 1)), 3)
        padded = pad_depth(rimmed).astype(jnp.float32)
        weight = adjoint.astype(jnp.float32)
        accumulated = accumulated + jnp.stack(
            [weight * sixth_order(padded, axis_id) for axis_id in range(3)]
        )
        got_landing, got_ops = arrivals[section_id]
        place_half, chosen_ops = sendlists[section_id]
        later_bricks = split_bricks(adjoint, edge_cells).reshape(brick_total, volume)
        at_slots = (got_landing[:, None] == brick_ids[None, :]).astype(jnp.bfloat16)
        wanted = jnp.dot(at_slots, later_bricks, preferred_element_type=jnp.float32).astype(
            jnp.bfloat16
        )
        pulled = apply_operator(
            lookup(operators, got_ops),
            wanted.reshape(slot_count, edge_cells, edge_cells * edge_cells),
            True,
        )
        pulled = pulled.astype(jnp.bfloat16).reshape(peer_count, capacity, volume)
        returned = lax.all_to_all(pulled, "gx", split_axis=0, concat_axis=0, tiled=True)
        own_bricks = jnp.dot(
            place_half.T, returned.reshape(slot_count, volume), preferred_element_type=jnp.float32
        ).astype(jnp.bfloat16)
        adjoint = join_bricks(
            own_bricks.reshape(brick_total, edge_cells, edge_cells * edge_cells), edge_cells
        )
    velocity_rim = extended(velocity.astype(jnp.bfloat16), (("gx", 1), ("gy", 2)), 3).astype(
        velocity.dtype
    )
    velocity_pad = pad_depth(velocity_rim)
    divergence = (
        sixth_order(velocity_pad[0], 0)
        + sixth_order(velocity_pad[1], 1)
        + sixth_order(velocity_pad[2], 2)
    )
    divergence_rim = extended(divergence.astype(jnp.bfloat16), (("gx", 0), ("gy", 1)), 3).astype(
        divergence.dtype
    )
    divergence_pad = pad_depth(divergence_rim)
    regular = jnp.stack([sixth_order(divergence_pad, axis_id) for axis_id in range(3)])
    velocity_grad = accumulated / STEPS - 0.25 * regular
    return (velocity_grad, adjoint)


def solution(mesh):
    placed = (
        P("gx", "gy", None),
        P("gx", "gy", None),
        P(None, "gx", "gy", None),
        P(),
        P(None, "gx", "gy", None, None),
        P(None, "gx", "gy", None),
        P(None, "gx", "gy", None),
    )
    return jax.shard_map(
        shards,
        mesh=mesh,
        in_specs=placed,
        out_specs=(P(None, "gx", "gy", None), P("gx", "gy", None)),
        check_vma=False,
    )
```

profile of v0, /device:TPU:1, one launch (start us, length us, event | category | flops | bytes accessed | tf_op | source)
XLA Modules:
  0.0 453.6 jit_solution(6335006604379599426)
XLA Ops:
  3.8 6.4 %all-to-all-start.3 = ((s32[8,1,2]{2,1,0:T(1,128)}), s32[8,1,2]{2,1,0:T(1,128)S(1)}, u32[]{:S(2)}, u32[]{:S(2)}) async-start(s32[8,1,2]{2,1,0:T(1,128)} %bitcast.8), calls=%async_computation.3 | async-start | bytes 8192 | tf_op jit(solution)/shard_map/all_to_all | solution.py:134
  74.9 7.7 %reshape.235 = f32[16,32,1024]{2,1,0:T(8,128)} reshape(f32[16,1024,32]{2,1,0:T(8,128)} %fusion.93) | data formatting | bytes 4194304 | tf_op jit(solution)/shard_map/reshape | solution.py:81
  82.6 10.1 %fusion.95 = f32[16,1024,32]{2,1,0:T(8,128)} fusion(f32[16,32,1024]{2,1,0:T(8,128)} %reshape.235, bf16[16,3,32,32]{3,2,1,0:T(8,128)(2,1)S(1)} %reshape.234), kind=kOutput, calls=%fused_computation.179 | convolution fusion | flops 201326592 | bytes 4325376 | tf_op jit(solution)/shard_map/mbr,myb->mry/dot_general | solution.py:82
  92.7 7.7 %reshape.236 = f32[16,32,1024]{2,1,0:T(8,128)} reshape(f32[16,1024,32]{2,1,0:T(8,128)} %fusion.95) | data formatting | bytes 4194304 | tf_op jit(solution)/shard_map/reshape | solution.py:85
  106.2 6.6 %convert_element_type.147 = bf16[16,32768]{1,0:T(8,128)(2,1)S(1)} reshape(bf16[16,1024,32]{2,1,0:T(8,128)(2,1)} %copy.104) | data formatting | bytes 2097152 | tf_op jit(solution)/shard_map/convert_element_type | solution.py:142
  118.1 12.9 %all-to-all-start.4 = ((bf16[8,2,32768]{2,1,0:T(2,128)(2,1)}), bf16[8,2,32768]{2,1,0:T(2,128)(2,1)}, u32[]{:S(2)}, u32[]{:S(2)}) async-start(bf16[8,2,32768]{2,1,0:T(2,128)(2,1)} %reshape.237), calls=%async_computation.4 | async-start | bytes 2097152 | tf_op jit(solution)/shard_map/all_to_all | solution.py:126
  163.4 9.1 %fusion.2 = f32[3,38,38,262]{3,2,1,0:T(8,128)} fusion(bf16[3,38,3,256]{3,2,1,0:T(4,128)(2,1)} %collective-permute-done.11, bf16[3,38,3,256]{3,2,1,0:T(4,128)(2,1)S(1)} %collective-permute-done.10, bf16[3,3,32,256]{3,2,1,0:T(8,128)(2,1)} %collective-permute-done.9, bf16[3,32,32,256]{3,2,1,0:T(8,128)(2,1)S(1)} %convert_element_type.171, ...), kind=kLoop, calls=%fused_computation.19 | loop fusion | flops 20429712 | bytes 6757920 | tf_op jit(solution)/shard_map/jit(_pad)/pad | solution.py:46
  182.0 7.7 %reshape.240 = f32[16,32,1024]{2,1,0:T(8,128)} reshape(f32[16,1024,32]{2,1,0:T(8,128)} %fusion.97) | data formatting | bytes 4194304 | tf_op jit(solution)/shard_map/reshape | solution.py:81
  189.7 10.1 %fusion.99 = f32[16,1024,32]{2,1,0:T(8,128)} fusion(f32[16,32,1024]{2,1,0:T(8,128)} %reshape.240, bf16[16,3,32,32]{3,2,1,0:T(8,128)(2,1)S(1)} %copy-done.14), kind=kOutput, calls=%fused_computation.183 | convolution fusion | flops 201326592 | bytes 4325376 | tf_op jit(solution)/shard_map/mbr,myb->mry/dot_general | solution.py:82
  199.8 7.9 %reshape.241 = f32[16,32,1024]{2,1,0:T(8,128)} reshape(f32[16,1024,32]{2,1,0:T(8,128)} %fusion.99) | data formatting | bytes 4194304 | tf_op jit(solution)/shard_map/reshape | solution.py:85
  216.0 6.8 %convert_element_type.152 = bf16[16,32768]{1,0:T(8,128)(2,1)} reshape(bf16[16,1024,32]{2,1,0:T(8,128)(2,1)} %copy.111) | data formatting | bytes 2097152 | tf_op jit(solution)/shard_map/convert_element_type | solution.py:142
  229.9 8.0 %copy.112 = f32[32,32,8,32]{3,2,1,0:T(8,128)} copy(f32[32,32,8,32]{3,1,0,2:T(8,128)} %bitcast.135) | data formatting | bytes 2097152 | tf_op jit(solution)/shard_map/convert_element_type | solution.py:156
  261.2 7.7 %reshape.245 = f32[16,32,1024]{2,1,0:T(8,128)} reshape(f32[16,1024,32]{2,1,0:T(8,128)} %fusion.96) | data formatting | bytes 4194304 | tf_op jit(solution)/shard_map/reshape | solution.py:81
  268.9 10.1 %fusion.98 = f32[16,1024,32]{2,1,0:T(8,128)} fusion(f32[16,32,1024]{2,1,0:T(8,128)} %reshape.245, bf16[16,3,32,32]{3,2,1,0:T(8,128)(2,1)S(1)} %copy-done.14), kind=kOutput, calls=%fused_computation.182 | convolution fusion | flops 201326592 | bytes 4325376 | tf_op jit(solution)/shard_map/mbr,mby->mry/dot_general | solution.py:82
  279.0 7.8 %reshape.246 = f32[16,32,1024]{2,1,0:T(8,128)} reshape(f32[16,1024,32]{2,1,0:T(8,128)} %fusion.98) | data formatting | bytes 4194304 | tf_op jit(solution)/shard_map/reshape | solution.py:85
  295.1 7.8 %convert_element_type.164 = bf16[8,2,32768]{2,1,0:T(2,128)(2,1)} reshape(bf16[16,1024,32]{2,1,0:T(8,128)(2,1)} %copy.122) | data formatting | bytes 2097152 | tf_op jit(solution)/shard_map/convert_element_type | solution.py:179
  349.7 7.7 %reshape.249 = f32[16,32,1024]{2,1,0:T(8,128)} reshape(f32[16,1024,32]{2,1,0:T(8,128)} %fusion.92) | data formatting | bytes 4194304 | tf_op jit(solution)/shard_map/reshape | solution.py:81
  357.4 10.1 %fusion.94 = f32[16,1024,32]{2,1,0:T(8,128)} fusion(f32[16,32,1024]{2,1,0:T(8,128)} %reshape.249, bf16[16,3,32,32]{3,2,1,0:T(8,128)(2,1)S(1)} %copy-done.13), kind=kOutput, calls=%fused_computation.178 | convolution fusion | flops 201326592 | bytes 4325376 | tf_op jit(solution)/shard_map/mbr,mby->mry/dot_general | solution.py:82
  367.6 7.7 %reshape.250 = f32[16,32,1024]{2,1,0:T(8,128)} reshape(f32[16,1024,32]{2,1,0:T(8,128)} %fusion.94) | data formatting | bytes 4194304 | tf_op jit(solution)/shard_map/reshape | solution.py:85
  383.6 7.8 %convert_element_type.176 = bf16[8,2,32768]{2,1,0:T(2,128)(2,1)} reshape(bf16[16,1024,32]{2,1,0:T(8,128)(2,1)} %copy.129) | data formatting | bytes 2097152 | tf_op jit(solution)/shard_map/convert_element_type | solution.py:179
  391.4 8.3 %all-to-all-start.7 = ((bf16[8,2,32768]{2,1,0:T(2,128)(2,1)}), bf16[8,2,32768]{2,1,0:T(2,128)(2,1)}, u32[]{:S(2)}, u32[]{:S(2)}) async-start(bf16[8,2,32768]{2,1,0:T(2,128)(2,1)} %convert_element_type.176), calls=%async_computation.7 | async-start | bytes 2097152 | tf_op jit(solution)/shard_map/all_to_all | solution.py:180
  399.8 13.7 %fusion.34 = (f32[1,32,32,256]{3,2,1,0:T(8,128)}, f32[1,32,32,256]{3,2,1,0:T(8,128)}, f32[1,32,32,256]{3,2,1,0:T(8,128)}) fusion(f32[38,38,256]{2,1,0:T(8,128)} %maximum_convert_fusion), kind=kLoop, calls=%fused_computation.78 | loop fusion | flops 6291456 | bytes 17285120 | tf_op jit(solution)/shard_map/stack | solution.py:200
  421.2 7.9 %copy.123 = f32[32,32,8,32]{3,2,1,0:T(8,128)} copy(f32[32,32,8,32]{3,1,0,2:T(8,128)} %bitcast.136) | data formatting | bytes 2097152 | tf_op jit(solution)/shard_map/convert_element_type | solution.py:163
  433.5 6.6 %fusion.73 = (f32[1,32,32,256]{3,2,1,0:T(8,128)S(1)}, f32[1,32,32,256]{3,2,1,0:T(8,128)S(1)}, f32[1,32,32,256]{3,2,1,0:T(8,128)S(1)}) fusion(f32[32,32,256]{2,1,0:T(8,128)} %reshape.254, f32[38,38,262]{2,1,0:T(8,128)S(1)} %copy-done.2), kind=kLoop, calls=%fused_computation.135 | loop fusion | flops 7077888 | bytes 23068672 | tf_op jit(solution)/shard_map/stack | solution.py:164
  (199 shorter events, 247.6 us)
Async XLA Ops:
  3.8 11.6 %all-to-all-start.3 = ((s32[8,1,2]{2,1,0:T(1,128)}), s32[8,1,2]{2,1,0:T(1,128)S(1)}, u32[]{:S(2)}, u32[]{:S(2)}) async-start(s32[8,1,2]{2,1,0:T(1,128)} %bitcast.8), calls=%async_computation.3 | async-start | bytes 8192 | tf_op jit(solution)/shard_map/all_to_all | solution.py:134
  16.0 9.8 %all-to-all-start.1 = ((s32[8,1,2]{2,1,0:T(1,128)}), s32[8,1,2]{2,1,0:T(1,128)S(1)}, u32[]{:S(2)}, u32[]{:S(2)}) async-start(s32[8,1,2]{2,1,0:T(1,128)} %bitcast.5), calls=%async_computation.1 | async-start | bytes 8192 | tf_op jit(solution)/shard_map/all_to_all | solution.py:133
  25.8 8.5 %all-to-all-start.5 = ((s32[8,1,2]{2,1,0:T(1,128)}), s32[8,1,2]{2,1,0:T(1,128)S(1)}, u32[]{:S(2)}, u32[]{:S(2)}) async-start(s32[8,1,2]{2,1,0:T(1,128)} %bitcast.14), calls=%async_computation.5 | async-start | bytes 8192 | tf_op jit(solution)/shard_map/all_to_all | solution.py:134
  34.3 8.5 %all-to-all-start = ((s32[8,1,2]{2,1,0:T(1,128)}), s32[8,1,2]{2,1,0:T(1,128)S(1)}, u32[]{:S(2)}, u32[]{:S(2)}) async-start(s32[8,1,2]{2,1,0:T(1,128)} %bitcast.2), calls=%async_computation | async-start | bytes 8192 | tf_op jit(solution)/shard_map/all_to_all | solution.py:133
  43.4 24.7 %all-to-all-start.2 = ((bf16[8,2,32768]{2,1,0:T(2,128)(2,1)}), bf16[8,2,32768]{2,1,0:T(2,128)(2,1)}, u32[]{:S(2)}, u32[]{:S(2)}) async-start(bf16[8,2,32768]{2,1,0:T(2,128)(2,1)} %reshape.231), calls=%async_computation.2 | async-start | bytes 2097152 | tf_op jit(solution)/shard_map/all_to_all | solution.py:126
  50.7 85.2 %collective-permute-start.8 = (bf16[3,3,32,256]{3,2,1,0:T(8,128)(2,1)}, bf16[3,3,32,256]{3,2,1,0:T(8,128)(2,1)S(1)}, u32[]{:S(2)}, u32[]{:S(2)}) collective-permute-start(bf16[3,3,32,256]{3,2,1,0:T(8,128)(2,1)} %get-tuple-element.20), channel_id=1, source_target_pairs={{0,4},{4,8},{8,12},{12,16},{16,20},{20,24},{24,28},{1,5},{5,9},{9,... | collective-permute-start | bytes 442376 | tf_op jit(solution)/shard_map/ppermute | solution.py:19
  53.9 82.0 %collective-permute-start.9 = (bf16[3,3,32,256]{3,2,1,0:T(8,128)(2,1)}, bf16[3,3,32,256]{3,2,1,0:T(8,128)(2,1)}, u32[]{:S(2)}, u32[]{:S(2)}) collective-permute-start(bf16[3,3,32,256]{3,2,1,0:T(8,128)(2,1)} %get-tuple-element.21), channel_id=1, source_target_pairs={{4,0},{8,4},{12,8},{16,12},{20,16},{24,20},{28,24},{5,1},{9,5},{13... | collective-permute-start | bytes 442376 | tf_op jit(solution)/shard_map/ppermute | solution.py:20
  55.2 10.8 %collective-permute-start.4 = (bf16[3,32,256]{2,1,0:T(8,128)(2,1)S(1)}, bf16[3,32,256]{2,1,0:T(8,128)(2,1)S(1)}, u32[]{:S(2)}, u32[]{:S(2)}) collective-permute-start(bf16[3,32,256]{2,1,0:T(8,128)(2,1)S(1)} %get-tuple-element.34), channel_id=1, source_target_pairs={{0,4},{4,8},{8,12},{12,16},{16,20},{20,24},{24,28},{1,5},{5,9},{9,... | collective-permute-start | bytes 147464 | tf_op jit(solution)/shard_map/ppermute | solution.py:19
  59.2 8.3 %collective-permute-start.5 = (bf16[3,32,256]{2,1,0:T(8,128)(2,1)S(1)}, bf16[3,32,256]{2,1,0:T(8,128)(2,1)S(1)}, u32[]{:S(2)}, u32[]{:S(2)}) collective-permute-start(bf16[3,32,256]{2,1,0:T(8,128)(2,1)S(1)} %get-tuple-element.33), channel_id=1, source_target_pairs={{4,0},{8,4},{12,8},{16,12},{20,16},{24,20},{28,24},{5,1},{9,5},{13... | collective-permute-start | bytes 147464 | tf_op jit(solution)/shard_map/ppermute | solution.py:20
  118.1 55.3 %all-to-all-start.4 = ((bf16[8,2,32768]{2,1,0:T(2,128)(2,1)}), bf16[8,2,32768]{2,1,0:T(2,128)(2,1)}, u32[]{:S(2)}, u32[]{:S(2)}) async-start(bf16[8,2,32768]{2,1,0:T(2,128)(2,1)} %reshape.237), calls=%async_computation.4 | async-start | bytes 2097152 | tf_op jit(solution)/shard_map/all_to_all | solution.py:126
  132.4 20.7 %collective-permute-start = (bf16[3,32,256]{2,1,0:T(8,128)(2,1)S(1)}, bf16[3,32,256]{2,1,0:T(8,128)(2,1)S(1)}, u32[]{:S(2)}, u32[]{:S(2)}) collective-permute-start(bf16[3,32,256]{2,1,0:T(8,128)(2,1)S(1)} %slice.346), channel_id=1, source_target_pairs={{0,4},{4,8},{8,12},{12,16},{16,20},{20,24},{24,28},{1,5},{5,9},{9,... | collective-permute-start | bytes 147464 | tf_op jit(solution)/shard_map/ppermute | solution.py:19
  136.9 26.5 %collective-permute-start.10 = (bf16[3,38,3,256]{3,2,1,0:T(4,128)(2,1)S(1)}, bf16[3,38,3,256]{3,2,1,0:T(4,128)(2,1)S(1)}, u32[]{:S(2)}, u32[]{:S(2)}) collective-permute-start(bf16[3,38,3,256]{3,2,1,0:T(4,128)(2,1)S(1)} %get-tuple-element.18), channel_id=1, source_target_pairs={{0,1},{1,2},{2,3},{4,5},{5,6},{6,7},{8,9},{9,10},{10,11},{12,13},{... | collective-permute-start | bytes 525320 | tf_op jit(solution)/shard_map/ppermute | solution.py:19
  142.7 20.7 %collective-permute-start.11 = (bf16[3,38,3,256]{3,2,1,0:T(4,128)(2,1)S(1)}, bf16[3,38,3,256]{3,2,1,0:T(4,128)(2,1)}, u32[]{:S(2)}, u32[]{:S(2)}) collective-permute-start(bf16[3,38,3,256]{3,2,1,0:T(4,128)(2,1)S(1)} %get-tuple-element.19), channel_id=1, source_target_pairs={{1,0},{2,1},{3,2},{5,4},{6,5},{7,6},{9,8},{10,9},{11,10},{13,12},{... | collective-permute-start | bytes 525320 | tf_op jit(solution)/shard_map/ppermute | solution.py:20
  151.8 4.8 %collective-permute-start.1 = (bf16[3,32,256]{2,1,0:T(8,128)(2,1)S(1)}, bf16[3,32,256]{2,1,0:T(8,128)(2,1)S(1)}, u32[]{:S(2)}, u32[]{:S(2)}) collective-permute-start(bf16[3,32,256]{2,1,0:T(8,128)(2,1)S(1)} %slice.348), channel_id=1, source_target_pairs={{4,0},{8,4},{12,8},{16,12},{20,16},{24,20},{28,24},{5,1},{9,5},{13... | collective-permute-start | bytes 147464 | tf_op jit(solution)/shard_map/ppermute | solution.py:20
  156.7 15.8 %collective-permute-start.2 = (bf16[38,3,256]{2,1,0:T(4,128)(2,1)S(1)}, bf16[38,3,256]{2,1,0:T(4,128)(2,1)S(1)}, u32[]{:S(2)}, u32[]{:S(2)}) collective-permute-start(bf16[38,3,256]{2,1,0:T(4,128)(2,1)S(1)} %get-tuple-element.29), channel_id=1, source_target_pairs={{0,1},{1,2},{2,3},{4,5},{5,6},{6,7},{8,9},{9,10},{10,11},{12,13},{... | collective-permute-start | bytes 175112 | tf_op jit(solution)/shard_map/ppermute | solution.py:19
  161.5 11.0 %collective-permute-start.3 = (bf16[38,3,256]{2,1,0:T(4,128)(2,1)S(1)}, bf16[38,3,256]{2,1,0:T(4,128)(2,1)S(1)}, u32[]{:S(2)}, u32[]{:S(2)}) collective-permute-start(bf16[38,3,256]{2,1,0:T(4,128)(2,1)S(1)} %get-tuple-element.30), channel_id=1, source_target_pairs={{1,0},{2,1},{3,2},{5,4},{6,5},{7,6},{9,8},{10,9},{11,10},{13,12},{... | collective-permute-start | bytes 175112 | tf_op jit(solution)/shard_map/ppermute | solution.py:20
  303.0 36.9 %all-to-all-start.6 = ((bf16[8,2,32768]{2,1,0:T(2,128)(2,1)}), bf16[8,2,32768]{2,1,0:T(2,128)(2,1)}, u32[]{:S(2)}, u32[]{:S(2)}) async-start(bf16[8,2,32768]{2,1,0:T(2,128)(2,1)} %convert_element_type.164), calls=%async_computation.6 | async-start | bytes 2097152 | tf_op jit(solution)/shard_map/all_to_all | solution.py:180
  316.8 12.2 %collective-permute-start.12 = (bf16[3,32,256]{2,1,0:T(8,128)(2,1)S(1)}, bf16[3,32,256]{2,1,0:T(8,128)(2,1)S(1)}, u32[]{:S(2)}, u32[]{:S(2)}) collective-permute-start(bf16[3,32,256]{2,1,0:T(8,128)(2,1)S(1)} %get-tuple-element.31), channel_id=1, source_target_pairs={{0,4},{4,8},{8,12},{12,16},{16,20},{20,24},{24,28},{1,5},{5,9},{9,... | collective-permute-start | bytes 147464 | tf_op jit(solution)/shard_map/ppermute | solution.py:19
  320.3 8.6 %collective-permute-start.13 = (bf16[3,32,256]{2,1,0:T(8,128)(2,1)S(1)}, bf16[3,32,256]{2,1,0:T(8,128)(2,1)S(1)}, u32[]{:S(2)}, u32[]{:S(2)}) collective-permute-start(bf16[3,32,256]{2,1,0:T(8,128)(2,1)S(1)} %get-tuple-element.32), channel_id=1, source_target_pairs={{4,0},{8,4},{12,8},{16,12},{20,16},{24,20},{28,24},{5,1},{9,5},{13... | collective-permute-start | bytes 147464 | tf_op jit(solution)/shard_map/ppermute | solution.py:20
  322.7 11.9 %collective-permute-start.6 = (bf16[38,3,256]{2,1,0:T(4,128)(2,1)S(1)}, bf16[38,3,256]{2,1,0:T(4,128)(2,1)S(1)}, u32[]{:S(2)}, u32[]{:S(2)}) collective-permute-start(bf16[38,3,256]{2,1,0:T(4,128)(2,1)S(1)} %get-tuple-element.27), channel_id=1, source_target_pairs={{0,1},{1,2},{2,3},{4,5},{5,6},{6,7},{8,9},{9,10},{10,11},{12,13},{... | collective-permute-start | bytes 175112 | tf_op jit(solution)/shard_map/ppermute | solution.py:19
  327.0 7.6 %collective-permute-start.7 = (bf16[38,3,256]{2,1,0:T(4,128)(2,1)S(1)}, bf16[38,3,256]{2,1,0:T(4,128)(2,1)S(1)}, u32[]{:S(2)}, u32[]{:S(2)}) collective-permute-start(bf16[38,3,256]{2,1,0:T(4,128)(2,1)S(1)} %get-tuple-element.28), channel_id=1, source_target_pairs={{1,0},{2,1},{3,2},{5,4},{6,5},{7,6},{9,8},{10,9},{11,10},{13,12},{... | collective-permute-start | bytes 175112 | tf_op jit(solution)/shard_map/ppermute | solution.py:20
  329.0 9.1 %collective-permute-start.14 = (bf16[38,3,256]{2,1,0:T(4,128)(2,1)S(1)}, bf16[38,3,256]{2,1,0:T(4,128)(2,1)S(1)}, u32[]{:S(2)}, u32[]{:S(2)}) collective-permute-start(bf16[38,3,256]{2,1,0:T(4,128)(2,1)S(1)} %get-tuple-element.25), channel_id=1, source_target_pairs={{0,1},{1,2},{2,3},{4,5},{5,6},{6,7},{8,9},{9,10},{10,11},{12,13},{... | collective-permute-start | bytes 175112 | tf_op jit(solution)/shard_map/ppermute | solution.py:19
  332.7 5.7 %collective-permute-start.15 = (bf16[38,3,256]{2,1,0:T(4,128)(2,1)S(1)}, bf16[38,3,256]{2,1,0:T(4,128)(2,1)S(1)}, u32[]{:S(2)}, u32[]{:S(2)}) collective-permute-start(bf16[38,3,256]{2,1,0:T(4,128)(2,1)S(1)} %get-tuple-element.26), channel_id=1, source_target_pairs={{1,0},{2,1},{3,2},{5,4},{6,5},{7,6},{9,8},{10,9},{11,10},{13,12},{... | collective-permute-start | bytes 175112 | tf_op jit(solution)/shard_map/ppermute | solution.py:20
  391.4 50.9 %all-to-all-start.7 = ((bf16[8,2,32768]{2,1,0:T(2,128)(2,1)}), bf16[8,2,32768]{2,1,0:T(2,128)(2,1)}, u32[]{:S(2)}, u32[]{:S(2)}) async-start(bf16[8,2,32768]{2,1,0:T(2,128)(2,1)} %convert_element_type.176), calls=%async_computation.7 | async-start | bytes 2097152 | tf_op jit(solution)/shard_map/all_to_all | solution.py:180
  (28 other events, 320.6 us)
where the time goes:
time: 462 us; the launch traced here: 454 us
  local copies, waits for them, and re-layouts  205 us (44%)
  starting transfers between devices  93.8 us (20%)
  matrix products  81.7 us (18%)
  other arithmetic  58.7 us (13%)
  waiting for transfers between devices  12.9 us (3%)
    dot_general x4, matrix products, apply_operator(): jnp.einsum(forms_list[1], view_one, matrices[:, 1].astype(jnp.float32), p...  40.5 us
    ppermute x8, starting transfers between devices, extended(): before = lax.ppermute(last, axis, up)  32.8 us
    reshape x4, local copies, waits for them, and re-layouts, apply_operator(): view_two = section_two.reshape(brick_total, edge_cells, square)  31.1 us
    reshape x4, local copies, waits for them, and re-layouts, apply_operator(): view_one = section_one.reshape(brick_total, edge_cells, square)  30.8 us
    convert_element_type x4, local copies, waits for them, and re-layouts, shards(): pulled = pulled.astype(jnp.bfloat16).reshape(peer_count, capacity, volume)  24.8 us
    convert_element_type x4, local copies, waits for them, and re-layouts, shards(): incoming = incoming.astype(jnp.bfloat16).reshape(slot_count, volume)  21.1 us
    dot_general x4, matrix products, apply_operator(): jnp.einsum(forms_list[0], bricks, matrices[:, 0], preferred_element_type=...  19.8 us
    all_to_all x2, starting transfers between devices, shards(): lax.all_to_all(packed.reshape(peer_count, capacity, volume), 'gx', split_...  17.2 us
  transfers between devices with their start and end apart: 24, of which 6 were waited for; matrix products, arithmetic and copies ran while one was open for 33% of the time, Pallas kernels for 0%

commit v1 on v0

v1 whole, which is shorter than its diff:
```python
import functools

import jax
import jax.numpy as jnp
from jax import lax
from jax.experimental import pallas as pl
from jax.experimental.pallas import tpu as pltpu
from jax.sharding import PartitionSpec as P

STEPS = 2
CAP = 2
RIM = 3
F32 = jnp.float32
BF16 = jnp.bfloat16
NT = (((1,), (1,)), ((), ()))
NN = (((1,), (0,)), ((), ()))
TAPS = ((1, 0.75), (2, -0.15), (3, 1.0 / 60.0))


def iota(shape, dim):
    return lax.broadcasted_iota(jnp.int32, shape, dim)


def mm(left, right, dims=NN):
    return lax.dot_general(left, right, dims, preferred_element_type=F32)


def halves(value):
    high = value.astype(BF16)
    return high, (value - high.astype(F32)).astype(BF16)


def spread_rows(operators, picks, axis):
    rows = jnp.concatenate([operators[pick, axis] for pick in picks], axis=0)
    edge = rows.shape[1]
    lanes = edge * len(picks)
    copies = (iota((edge, lanes), 1) % edge == iota((edge, lanes), 0)).astype(F32).astype(BF16)
    return mm(rows, copies)


def same_block(size, edge):
    return iota((size, size), 0) // edge == iota((size, size), 1) // edge


def block_diagonal(spread, edge, flipped):
    size = spread.shape[0]
    matrix = jnp.where(same_block(size, edge), spread, 0.0).astype(BF16)
    if flipped:
        one = (iota((size, size), 0) == iota((size, size), 1)).astype(F32).astype(BF16)
        matrix = mm(one, matrix, NT).astype(BF16)
    return matrix


def swap_chunks(parts):
    lane = iota(parts[0].shape, 1)
    for bit, shift in ((1, 32), (2, 64)):
        keep = (lane & shift) == 0
        fresh = list(parts)
        for index in range(4):
            if index & bit:
                continue
            one, two = parts[index], parts[index | bit]
            fresh[index] = jnp.where(keep, one, pltpu.roll(two, shift, 1))
            fresh[index | bit] = jnp.where(keep, pltpu.roll(one, 128 - shift, 1), two)
        parts = fresh
    return parts


def swap_brick(block, folded, turned, brick):
    slabs = []
    for ph in range(4):
        slabs.append(
            jnp.concatenate(
                [
                    block[(qs // 2) * 32 + ph * 8 : (qs // 2) * 32 + ph * 8 + 8, (qs % 2) * 128 : (qs % 2) * 128 + 128]
                    for qs in range(8)
                ],
                axis=0,
            )
        )
    slabs = swap_chunks(slabs)
    for qh in range(4):
        folded[brick * 4 + qh] = slabs[qh]
    for ps in range(8):
        value = jnp.concatenate(
            [folded[brick * 4 + qh, pl.ds(ps, 8, stride=8), :] for qh in range(4)], axis=0
        )
        turned[brick * 32 : brick * 32 + 32, ps * 128 : ps * 128 + 128] = value


def middle_and_last(start, spread_mid, last, folded, turned, flipped):
    size = spread_mid.shape[0]
    bricks = size // 32
    mask = same_block(size, 32)
    for brick in range(bricks):
        rows = spread_mid[brick * 32 : brick * 32 + 32]
        line = jnp.where(mask, jnp.concatenate([rows] * 8, axis=0), 0.0).astype(BF16)
        block = start[brick * 32 : brick * 32 + 32, :]
        block = jnp.concatenate([block[:, g * 256 : g * 256 + 256] for g in range(4)], axis=0)
        high, low = halves(block)
        both = mm(jnp.concatenate([high, low], axis=0), line, NN if flipped else NT)
        swap_brick(both[:128] + both[128:], folded, turned, brick)
    out = []
    for g in range(4):
        high, low = halves(turned[:, g * 256 : g * 256 + 256])
        out.append(mm(last, high) + mm(last, low))
    return out


def slot_numbers(route, step, bricks):
    own = [route[step, 0, 0, b, 0] for b in range(bricks)]
    slots = []
    for b in range(bricks):
        rank = jnp.int32(0)
        for other in range(b):
            rank = rank + (own[other] == own[b]).astype(jnp.int32)
        slots.append(own[b] * CAP + rank)
    return slots


def forward_kernel(step, first, last, from_native, *refs):
    if from_native:
        picks, route, operators, field, send, start, folded, turned = refs
    else:
        picks, route, landing, operators, arrived, send, field, start, folded, turned, total = refs
    bricks = 8
    chosen = [picks[step, 0, 0, b] for b in range(bricks)]
    slots = slot_numbers(route, step, bricks)
    begin = block_diagonal(spread_rows(operators, chosen, first), 32, False)
    if from_native:
        for g in range(4):
            block = jnp.concatenate(
                [field[qh * 8 + qs] for qs in (2 * g, 2 * g + 1) for qh in range(4)], axis=0
            )
            start[:, g * 256 : g * 256 + 256] = mm(begin, block, NT)
    else:
        gather_sum(step - 1, landing, arrived, total)
        field[...] = total[...].astype(BF16)
        stored = field[...].reshape(256, 1024)
        for g in range(4):
            start[:, g * 256 : g * 256 + 256] = mm(begin, stored[:, g * 256 : g * 256 + 256])
    spread_mid = spread_rows(operators, chosen, 1)
    end = block_diagonal(spread_rows(operators, chosen, last), 32, False)
    out = middle_and_last(start, spread_mid, end, folded, turned, False)
    for g in range(4):
        moved = out[g].astype(BF16)
        for b in range(bricks):
            send[slots[b], :, g * 256 : g * 256 + 256] = moved[b * 32 : b * 32 + 32]


def gather_sum(step, landing, arrived, total):
    total[...] = jnp.zeros(total.shape, F32)

    def add(slot, carry):
        brick = landing[step, slot]

        @pl.when(brick >= 0)
        def _():
            total[brick] = total[brick] + arrived[slot].astype(F32)

        return carry

    lax.fori_loop(0, arrived.shape[0], add, 0)


def hand_out(step, landing, field, send):
    def put(slot, carry):
        brick = landing[step, slot]

        @pl.when(brick >= 0)
        def _():
            send[slot] = field[brick]

        return carry

    lax.fori_loop(0, send.shape[0], put, 0)


def residual_kernel(landing, arrived, target, send, adjoint, total):
    gather_sum(1, landing, arrived, total)
    for b in range(8):
        final = total[b].astype(BF16).astype(F32)
        adjoint[b] = (final - target[b].astype(F32)).astype(BF16)
    hand_out(1, landing, adjoint, send)


def backward_kernel(step, first, last, *refs):
    if step:
        picks, route, landing, operators, arrived, send, adjoint, start, folded, turned = refs
    else:
        picks, route, operators, arrived, adjoint, start, folded, turned = refs
    bricks = 8
    chosen = [picks[step, 0, 0, b] for b in range(bricks)]
    slots = slot_numbers(route, step, bricks)
    begin = block_diagonal(spread_rows(operators, chosen, first), 32, True)
    stored = jnp.concatenate([arrived[slots[b]] for b in range(bricks)], axis=0)
    for g in range(4):
        start[:, g * 256 : g * 256 + 256] = mm(begin, stored[:, g * 256 : g * 256 + 256])
    spread_mid = spread_rows(operators, chosen, 1)
    end = block_diagonal(spread_rows(operators, chosen, last), 32, True)
    out = middle_and_last(start, spread_mid, end, folded, turned, True)
    if step:
        for g in range(4):
            moved = out[g].astype(BF16)
            for b in range(bricks):
                adjoint[b, :, g * 256 : g * 256 + 256] = moved[b * 32 : b * 32 + 32]
        hand_out(0, landing, adjoint, send)
    else:
        for g in range(4):
            to_native(out[g].astype(BF16), g, adjoint)


def to_native(block, g, field):
    size = block.shape[0]
    one = (iota((size, size), 0) == iota((size, size), 1)).astype(F32).astype(BF16)
    flat = mm(one, block, NT).astype(field.dtype)
    for index in range(8):
        x = (index % 4) * 8 + 2 * g + index // 4
        field[x] = flat[index * 32 : index * 32 + 32]


def x_form_to_native(source, folded, turned, field):
    for b in range(8):
        block = source[b].astype(F32)
        block = jnp.concatenate([block[:, g * 256 : g * 256 + 256] for g in range(4)], axis=0)
        swap_brick(block, folded, turned, b)
    for g in range(4):
        to_native(turned[:, g * 256 : g * 256 + 256].astype(BF16), g, field)


def tap(offset):
    value = jnp.zeros(offset.shape, F32)
    for step, weight in TAPS:
        value = jnp.where(offset == step, weight, value)
        value = jnp.where(offset == -step, -weight, value)
    return value


def stencils():
    size = 256
    row, col = iota((size, size), 0), iota((size, size), 1)
    along_y = halves(jnp.where(row // 32 == col // 32, tap(col - row), 0.0))
    along_z = halves(tap(row - col))
    row, col = iota((size, 48), 0), iota((size, 48), 1)
    layer = col // 8
    place = jnp.where(layer < RIM, layer - RIM, layer - RIM + 32)
    rim_y = halves(jnp.where(row // 32 == col % 8, tap(place - row % 32), 0.0))
    return along_y, rim_y, along_z


def rim_picker():
    row, col = iota((48, 256), 0), iota((48, 256), 1)
    layer = row // 8
    place = jnp.where(layer < RIM, layer, layer - RIM + 29)
    return ((row % 8 == col // 32) & (place == col % 32)).astype(F32).astype(BF16)


def difference_x(padded, g):
    total = None
    for step, weight in TAPS:
        ahead = padded[pl.ds(8 * g + RIM + step, 8)]
        behind = padded[pl.ds(8 * g + RIM - step, 8)]
        term = weight * (ahead - behind)
        total = term if total is None else total + term
    return total.reshape(256, 256)


def difference_y(parts, rims, along_y, rim_y):
    total = mm(along_y[0], parts[0]) + mm(along_y[1], parts[0])
    if len(parts) > 1:
        total = total + mm(along_y[0], parts[1])
    return total + mm(rim_y[0], rims) + mm(rim_y[1], rims)


def difference_z(parts, along_z):
    total = mm(parts[0], along_z[0]) + mm(parts[0], along_z[1])
    if len(parts) > 1:
        total = total + mm(parts[1], along_z[0])
    return total


def rim_rows(before, after, base, g):
    rows = [before[base + h, (g // 2) * 16 : (g // 2) * 16 + 16, :].astype(F32) for h in range(RIM)]
    rows += [after[base + h, (g // 2) * 16 : (g // 2) * 16 + 16, :].astype(F32) for h in range(RIM)]
    half = (g % 2) * 8
    return jnp.concatenate([value[half : half + 8] for value in rows], axis=0).astype(BF16)


def put_rims(blocks, base, low_y, high_y):
    picker = rim_picker()
    for pair in range(2):
        left, right = mm(picker, blocks[2 * pair]), mm(picker, blocks[2 * pair + 1])
        for layer in range(2 * RIM):
            value = jnp.concatenate(
                [left[layer * 8 : layer * 8 + 8], right[layer * 8 : layer * 8 + 8]], axis=0
            ).astype(BF16)
            target = low_y if layer < RIM else high_y
            target[base + layer % RIM, pair * 16 : pair * 16 + 16, :] = value


def opening_kernel(template, target, first_x, last_x, mid_v, low_x, high_x, low_y, high_y, target_z):
    low_x[0:RIM] = template[0:RIM]
    high_x[0:RIM] = template[29:32]
    low_x[RIM : 2 * RIM] = first_x[0, 0:RIM].astype(BF16)
    high_x[RIM : 2 * RIM] = last_x[0, 1:4].astype(BF16)
    put_rims([template[8 * g : 8 * g + 8].reshape(256, 256) for g in range(4)], 0, low_y, high_y)
    put_rims([mid_v[0, 8 * g : 8 * g + 8].astype(BF16).reshape(256, 256) for g in range(4)], RIM, low_y, high_y)
    one = (iota((256, 256), 0) == iota((256, 256), 1)).astype(F32).astype(BF16)
    for g in range(4):
        block = jnp.concatenate(
            [target[qh * 8 + qs] for qs in (2 * g, 2 * g + 1) for qh in range(4)], axis=0
        )
        flat = mm(one, block, NT).astype(BF16)
        for b in range(8):
            target_z[b, :, g * 256 : g * 256 + 256] = flat[b * 32 : b * 32 + 32]


def divergence_kernel(velocity, before_x, after_x, before_y, after_y, divergence, padded):
    along_y, rim_y, along_z = stencils()
    padded[0:RIM] = before_x[RIM : 2 * RIM].astype(F32)
    padded[RIM : RIM + 32] = velocity[0]
    padded[RIM + 32 : 2 * RIM + 32] = after_x[RIM : 2 * RIM].astype(F32)
    for g in range(4):
        along_one = halves(velocity[1, 8 * g : 8 * g + 8].reshape(256, 256))
        along_two = halves(velocity[2, 8 * g : 8 * g + 8].reshape(256, 256))
        total = (
            difference_x(padded, g)
            + difference_y(along_one, rim_rows(before_y, after_y, RIM, g), along_y, rim_y)
            + difference_z(along_two, along_z)
        )
        divergence[8 * g : 8 * g + 8] = total.reshape(8, 32, 256)


def rims_kernel(state, divergence, native, low_x, high_x, low_y, high_y, folded, turned):
    x_form_to_native(state, folded, turned, native)
    low_x[0:RIM] = native[0:RIM]
    high_x[0:RIM] = native[29:32]
    low_x[RIM : 2 * RIM] = divergence[0:RIM].astype(BF16)
    high_x[RIM : 2 * RIM] = divergence[29:32].astype(BF16)
    put_rims([native[8 * g : 8 * g + 8].reshape(256, 256) for g in range(4)], 0, low_y, high_y)
    put_rims(
        [divergence[8 * g : 8 * g + 8].astype(BF16).reshape(256, 256) for g in range(4)], RIM, low_y, high_y
    )


def gradient_kernel(
    template,
    state,
    divergence,
    adjoint_two,
    adjoint_one,
    b0x,
    a0x,
    b0y,
    a0y,
    b1x,
    a1x,
    b1y,
    a1y,
    gradient,
    folded,
    turned,
    weight_two,
    weight_one,
    pad_zero,
    pad_one,
    pad_div,
):
    x_form_to_native(adjoint_one, folded, turned, weight_one)
    stored = adjoint_two[...].reshape(256, 1024)
    for g in range(4):
        to_native(stored[:, g * 256 : g * 256 + 256], g, weight_two)
    along_y, rim_y, along_z = stencils()
    for padded, before, middle, after, base in (
        (pad_zero, b0x, template, a0x, 0),
        (pad_one, b1x, state, a1x, 0),
        (pad_div, b1x, divergence, a1x, RIM),
    ):
        padded[0:RIM] = before[base : base + RIM].astype(F32)
        padded[RIM : RIM + 32] = middle[...].astype(F32)
        padded[RIM + 32 : 2 * RIM + 32] = after[base : base + RIM].astype(F32)
    for g in range(4):
        zero = (template[8 * g : 8 * g + 8].reshape(256, 256),)
        one = (state[8 * g : 8 * g + 8].reshape(256, 256),)
        div = halves(divergence[8 * g : 8 * g + 8].reshape(256, 256))
        weigh_one = 0.5 * weight_one[8 * g : 8 * g + 8].reshape(256, 256)
        weigh_two = 0.5 * weight_two[8 * g : 8 * g + 8].reshape(256, 256)
        for axis in range(3):
            if axis == 0:
                parts = [difference_x(padded, g) for padded in (pad_zero, pad_one, pad_div)]
            elif axis == 1:
                parts = [
                    difference_y(zero, rim_rows(b0y, a0y, 0, g), along_y, rim_y),
                    difference_y(one, rim_rows(b1y, a1y, 0, g), along_y, rim_y),
                    difference_y(div, rim_rows(b1y, a1y, RIM, g), along_y, rim_y),
                ]
            else:
                parts = [difference_z(value, along_z) for value in (zero, one, div)]
            value = weigh_one * parts[0] + weigh_two * parts[1] - 0.25 * parts[2]
            gradient[axis, 8 * g : 8 * g + 8] = value.reshape(8, 32, 256)


def plan_kernel(codes, landing):
    me = lax.axis_index("gx")
    for step in range(STEPS):

        def row(source, carry):
            for slot in range(CAP):
                landing[step, source * CAP + slot] = jnp.int32(-1)
            rank = jnp.int32(0)
            for b in range(8):
                code = codes[source, step * 8 + b]
                hit = (code >> 3) == me

                @pl.when(hit)
                def _():
                    landing[step, source * CAP + rank] = code & 7

                rank = rank + hit.astype(jnp.int32)
            return carry

        lax.fori_loop(0, codes.shape[0], row, 0)


SCALAR = pl.BlockSpec(memory_space=pltpu.SMEM)
WHOLE = pl.BlockSpec(memory_space=pltpu.VMEM)
FOLDED = (32, 64, 128)
FLAT = (256, 1024)
NATIVE = (32, 32, 256)
FORM = (8, 32, 1024)


def call(kernel, out, specs, scratch, cost):
    many = isinstance(out, (list, tuple))
    return pl.pallas_call(
        kernel,
        out_shape=out,
        in_specs=specs,
        out_specs=[WHOLE] * len(out) if many else WHOLE,
        scratch_shapes=scratch,
        compiler_params=pltpu.CompilerParams(vmem_limit_bytes=48 * 1024 * 1024),
        cost_estimate=pl.CostEstimate(flops=cost, bytes_accessed=8 * 1024 * 1024, transcendentals=0),
    )


def like(shape, dtype):
    return jax.ShapeDtypeStruct(shape, dtype)


def neighbours(low_x, high_x, low_y, high_y):
    moved = []
    for low, high, axis in ((low_x, high_x, "gx"), (low_y, high_y, "gy")):
        size = lax.axis_size(axis)
        up = [(i, i + 1) for i in range(size - 1)]
        down = [(i + 1, i) for i in range(size - 1)]
        moved += [lax.ppermute(high, axis, up), lax.ppermute(low, axis, down)]
    return moved


def swap_slots(send):
    return lax.all_to_all(send, "gx", split_axis=0, concat_axis=0, tiled=True)


def shards(template, target_image, velocity, operators, route, target_brick, operator_index):
    peers = lax.axis_size("gx")
    slots = like((peers * CAP, 32, 1024), BF16)
    turning = [pltpu.VMEM(FLAT, F32), pltpu.VMEM(FOLDED, F32), pltpu.VMEM(FLAT, F32)]
    total = [pltpu.VMEM(FORM, F32)]
    work = 1 << 31

    codes = (route[:, 0, 0, :, 0] * 8 + target_brick[:, 0, 0]).reshape(STEPS * 8)
    codes = lax.all_gather(codes, "gx")
    landing = pl.pallas_call(
        plan_kernel,
        out_shape=like((STEPS, peers * CAP), jnp.int32),
        in_specs=[SCALAR],
        out_specs=SCALAR,
    )(codes)

    send = call(
        functools.partial(forward_kernel, 0, 2, 0, True), slots, [SCALAR, SCALAR, WHOLE, WHOLE], turning, work
    )(operator_index, route, operators, template)
    arrived = swap_slots(send)

    rim = like((2 * RIM, 32, 256), BF16)
    low_x, high_x, low_y, high_y, target_z = pl.pallas_call(
        opening_kernel,
        out_shape=[rim] * 4 + [like(FORM, BF16)],
        grid=(1,),
        in_specs=[
            pl.BlockSpec(NATIVE, lambda i: (0, 0, 0)),
            pl.BlockSpec(NATIVE, lambda i: (0, 0, 0)),
            pl.BlockSpec((1, 4, 32, 256), lambda i: (0, 0, 0, 0)),
            pl.BlockSpec((1, 4, 32, 256), lambda i: (0, 7, 0, 0)),
            pl.BlockSpec((1, 32, 32, 256), lambda i: (1, 0, 0, 0)),
        ],
        out_specs=[pl.BlockSpec((2 * RIM, 32, 256), lambda i: (0, 0, 0))] * 4
        + [pl.BlockSpec(FORM, lambda i: (0, 0, 0))],
        compiler_params=pltpu.CompilerParams(vmem_limit_bytes=48 * 1024 * 1024),
        cost_estimate=pl.CostEstimate(flops=work, bytes_accessed=8 * 1024 * 1024, transcendentals=0),
    )(template, target_image, velocity, velocity, velocity)
    b0x, a0x, b0y, a0y = neighbours(low_x, high_x, low_y, high_y)
    divergence = call(
        divergence_kernel, like(NATIVE, F32), [WHOLE] * 5, [pltpu.VMEM((38, 32, 256), F32)], work
    )(velocity, b0x, a0x, b0y, a0y)

    send, state_x = call(
        functools.partial(forward_kernel, 1, 0, 2, False),
        [slots, like(FORM, BF16)],
        [SCALAR, SCALAR, SCALAR, WHOLE, WHOLE],
        turning + total,
        work,
    )(operator_index, route, landing, operators, arrived)
    arrived = swap_slots(send)

    state, low_x, high_x, low_y, high_y = call(
        rims_kernel,
        [like(NATIVE, BF16)] + [rim] * 4,
        [WHOLE] * 2,
        turning[1:],
        work,
    )(state_x, divergence)
    b1x, a1x, b1y, a1y = neighbours(low_x, high_x, low_y, high_y)

    send, adjoint_two = call(
        residual_kernel, [slots, like(FORM, BF16)], [SCALAR, WHOLE, WHOLE], total, work
    )(landing, arrived, target_z)
    arrived = swap_slots(send)

    send, adjoint_one = call(
        functools.partial(backward_kernel, 1, 2, 0),
        [slots, like(FORM, BF16)],
        [SCALAR, SCALAR, SCALAR, WHOLE, WHOLE],
        turning,
        work,
    )(operator_index, route, landing, operators, arrived)
    arrived = swap_slots(send)

    gradient = call(
        gradient_kernel,
        like((3,) + NATIVE, F32),
        [WHOLE] * 13,
        turning[1:] + [pltpu.VMEM(NATIVE, F32)] * 2 + [pltpu.VMEM((38, 32, 256), F32)] * 3,
        work,
    )(template, state, divergence, adjoint_two, adjoint_one, b0x, a0x, b0y, a0y, b1x, a1x, b1y, a1y)

    adjoint = call(
        functools.partial(backward_kernel, 0, 0, 2),
        like(NATIVE, BF16),
        [SCALAR, SCALAR, WHOLE, WHOLE],
        turning,
        work,
    )(operator_index, route, operators, arrived)
    return gradient, adjoint


def solution(mesh):
    placed = (
        P("gx", "gy", None),
        P("gx", "gy", None),
        P(None, "gx", "gy", None),
        P(),
        P(None, "gx", "gy", None, None),
        P(None, "gx", "gy", None),
        P(None, "gx", "gy", None),
    )
    return jax.shard_map(
        shards,
        mesh=mesh,
        in_specs=placed,
        out_specs=(P(None, "gx", "gy", None), P("gx", "gy", None)),
        check_vma=False,
    )
```

time: 462 us -> 181 us (0.39)
  the two profiles are of different devices: /device:TPU:1 before, /device:TPU:17 now
where the time goes in v1:
time: 181 us; the launch traced here: 180 us
  blocking collectives  59.5 us (33%)
  starting transfers between devices  42.6 us (24%)
  waiting for transfers between devices  34.1 us (19%)
  Pallas kernels  26.6 us (15%)
  local copies, waits for them, and re-layouts  15.1 us (8%)
    all_to_all x1, blocking collectives, swap_slots(): return lax.all_to_all(send, 'gx', split_axis=0, concat_axis=0, tiled=True)  30.8 us
    all_gather x1, blocking collectives, shards(): codes = lax.all_gather(codes, 'gx')  28.7 us
    ppermute x8, starting transfers between devices, neighbours(): moved += [lax.ppermute(high, axis, up), lax.ppermute(low, axis, down)]  26.3 us
    all_to_all x3, waiting for transfers between devices, swap_slots(): return lax.all_to_all(send, 'gx', split_axis=0, concat_axis=0, tiled=True)  17.2 us
    ppermute x8, waiting for transfers between devices, neighbours(): moved += [lax.ppermute(high, axis, up), lax.ppermute(low, axis, down)]  16.9 us
    all_to_all x3, starting transfers between devices, swap_slots(): return lax.all_to_all(send, 'gx', split_axis=0, concat_axis=0, tiled=True)  16.3 us
    unnamed x53, local copies, waits for them, and re-layouts  14.9 us
    pallas_call x1, Pallas kernels, shards(): call(gradient_kernel, like((3,) + NATIVE, F32), [WHOLE] * 13, turning[1:]...  5.84 us
  transfers between devices with their start and end apart: 11, of which 3 were waited for; matrix products, arithmetic and copies ran while one was open for 1% of the time, Pallas kernels for 6%

profile of v1, /device:TPU:17, one launch (start us, length us, event | category | flops | bytes accessed | tf_op | source)
XLA Modules:
  0.0 179.6 jit_solution(6340614703377043948)
XLA Ops:
  1.4 2.3 %copy.20.refs_2_.refs_3_ = bf16[64,3,32,32]{3,2,1,0:T(8,128)(2,1)S(1)} copy(bf16[64,3,32,32]{0,3,2,1:T(8,128)(2,1)} %param.10) | data formatting | bytes 786432 | tf_op args[3]
  5.4 3.4 %shard_map.87 = bf16[16,32,1024]{2,1,0:T(8,128)(2,1)} custom-call(s32[2,1,1,8]{3,2,1,0:T(1,128)S(1)} %copy-done.15, s32[2,1,1,8,1]{4,3,2,1,0:T(8,128)S(1)} %copy.19.refs_1_, bf16[64,3,32,32]{3,2,1,0:T(8,128)(2,1)S(1)} %copy.20.refs_2_.refs_3_, bf16[32,32,256]{2,1,0:T(8,128)(2,1)S(1)} %copy-done.8), custom_call_target="tpu_custom_call" | custom-call | flops 2147483648 | bytes 8388608 | tf_op jit(solution)/shard_map/pallas_call | solution.py:480
  8.8 5.6 %all-to-all-start = ((bf16[16,32,1024]{2,1,0:T(8,128)(2,1)}), bf16[16,32,1024]{2,1,0:T(8,128)(2,1)}, u32[]{:S(2)}, u32[]{:S(2)}) async-start(bf16[16,32,1024]{2,1,0:T(8,128)(2,1)} %shard_map.87), calls=%async_computation | async-start | bytes 2097152 | tf_op jit(solution)/shard_map/all_to_all | solution.py:461
  15.8 28.7 %all-gather = s32[8,1,16]{2,1,0:T(1,128)} all-gather(s32[1,1,16]{2,1,0:T(1,128)S(1)} %add_bitcast_fusion), channel_id=1, replica_groups=mesh['gx'=8,'gy'=4] {'gx'}, dimensions={0}, use_global_device_ids=true | all-gather | bytes 576 | tf_op jit(solution)/shard_map/all_gather | solution.py:472
  44.5 1.8 %shard_map.86.refs_2_.landing = s32[2,16]{1,0:T(2,128)} custom-call(s32[8,16]{1,0:T(8,128)} %bitcast.3), custom_call_target="tpu_custom_call" | custom-call | tf_op jit(solution)/shard_map/pallas_call | solution.py:473
  48.6 3.4 %shard_map.88 = (bf16[16,32,1024]{2,1,0:T(8,128)(2,1)S(1)}, bf16[8,32,1024]{2,1,0:T(8,128)(2,1)S(1)}) custom-call(s32[2,1,1,8]{3,2,1,0:T(1,128)S(1)} %copy-done.16, s32[2,1,1,8,1]{4,3,2,1,0:T(8,128)S(1)} %copy.19.refs_1_, s32[2,16]{1,0:T(2,128)S(1)} %copy-done.11, bf16[64,3,32,32]{3,2,1,0:T(8,128)(2,1)S(1)} %copy-done.2, ...), custom_call_target="tpu_custom_call" | custom-call | flops 2147483648 | bytes 8388608 | tf_op jit(solution)/shard_map/pallas_call | solution.py:507
  53.7 5.1 %all-to-all-start.1 = ((bf16[16,32,1024]{2,1,0:T(8,128)(2,1)}), bf16[16,32,1024]{2,1,0:T(8,128)(2,1)}, u32[]{:S(2)}, u32[]{:S(2)}) async-start(bf16[16,32,1024]{2,1,0:T(8,128)(2,1)} %copy-done.6), calls=%async_computation.1 | async-start | bytes 2097152 | tf_op jit(solution)/shard_map/all_to_all | solution.py:461
  62.3 17.2 %all-to-all-done.1.arrived = bf16[16,32,1024]{2,1,0:T(8,128)(2,1)} async-done(((bf16[16,32,1024]{2,1,0:T(8,128)(2,1)}), bf16[16,32,1024]{2,1,0:T(8,128)(2,1)}, u32[]{:S(2)}, u32[]{:S(2)}) %all-to-all-start.1) | async-done | bytes 1048608 | tf_op jit(solution)/shard_map/all_to_all | solution.py:461
  80.5 2.2 %shard_map.92 = (bf16[16,32,1024]{2,1,0:T(8,128)(2,1)S(1)}, bf16[8,32,1024]{2,1,0:T(8,128)(2,1)S(1)}) custom-call(s32[2,16]{1,0:T(2,128)S(1)} %copy-done.12, bf16[16,32,1024]{2,1,0:T(8,128)(2,1)} %all-to-all-done.1.arrived, bf16[8,32,1024]{2,1,0:T(8,128)(2,1)S(1)} %copy-done.14), custom_call_target="tpu_custom_call" | custom-call | flops 2147483648 | bytes 8388608 | tf_op jit(solution)/shard_map/pallas_call | solution.py:525
  82.7 30.8 %all_to_all.20.refs_4_ = bf16[16,32,1024]{2,1,0:T(8,128)(2,1)S(1)} all-to-all(bf16[16,32,1024]{2,1,0:T(8,128)(2,1)S(1)} %get-tuple-element.27), channel_id=1, replica_groups=mesh['gx'=8,'gy'=4] {'gx'}, dimensions={0} | all-to-all | bytes 2097152 | tf_op jit(solution)/shard_map/all_to_all | solution.py:461
  113.5 2.9 %shard_map.93 = (bf16[16,32,1024]{2,1,0:T(8,128)(2,1)S(1)}, bf16[8,32,1024]{2,1,0:T(8,128)(2,1)S(1)}) custom-call(s32[2,1,1,8]{3,2,1,0:T(1,128)S(1)} %copy-done.16, s32[2,1,1,8,1]{4,3,2,1,0:T(8,128)S(1)} %copy.19.refs_1_, s32[2,16]{1,0:T(2,128)S(1)} %copy-done.12, bf16[64,3,32,32]{3,2,1,0:T(8,128)(2,1)S(1)} %copy-done.3, ...), custom_call_target="tpu_custom_call" | custom-call | flops 2147483648 | bytes 8388608 | tf_op jit(solution)/shard_map/pallas_call | solution.py:530
  118.1 5.5 %all-to-all-start.3 = ((bf16[16,32,1024]{2,1,0:T(8,128)(2,1)}), bf16[16,32,1024]{2,1,0:T(8,128)(2,1)}, u32[]{:S(2)}, u32[]{:S(2)}) async-start(bf16[16,32,1024]{2,1,0:T(8,128)(2,1)} %copy-done.5), calls=%async_computation.3 | async-start | bytes 2097152 | tf_op jit(solution)/shard_map/all_to_all | solution.py:461
  123.7 3.1 %collective-permute-start = (bf16[6,32,256]{2,1,0:T(8,128)(2,1)S(1)}, bf16[6,32,256]{2,1,0:T(8,128)(2,1)S(1)}, u32[]{:S(2)}, u32[]{:S(2)}) collective-permute-start(bf16[6,32,256]{2,1,0:T(8,128)(2,1)S(1)} %get-tuple-element.19), channel_id=1, source_target_pairs={{0,4},{4,8},{8,12},{12,16},{16,20},{20,24},{24,28},{1,5},{5,9},{9,... | collective-permute-start | bytes 294920 | tf_op jit(solution)/shard_map/ppermute | solution.py:456
  126.8 3.1 %collective-permute-start.1 = (bf16[6,32,256]{2,1,0:T(8,128)(2,1)S(1)}, bf16[6,32,256]{2,1,0:T(8,128)(2,1)S(1)}, u32[]{:S(2)}, u32[]{:S(2)}) collective-permute-start(bf16[6,32,256]{2,1,0:T(8,128)(2,1)S(1)} %get-tuple-element.20), channel_id=1, source_target_pairs={{4,0},{8,4},{12,8},{16,12},{20,16},{24,20},{28,24},{5,1},{9,5},{13... | collective-permute-start | bytes 294920 | tf_op jit(solution)/shard_map/ppermute | solution.py:456
  129.9 5.8 %collective-permute-start.2 = (bf16[6,32,256]{2,1,0:T(8,128)(2,1)S(1)}, bf16[6,32,256]{2,1,0:T(8,128)(2,1)S(1)}, u32[]{:S(2)}, u32[]{:S(2)}) collective-permute-start(bf16[6,32,256]{2,1,0:T(8,128)(2,1)S(1)} %get-tuple-element.21), channel_id=1, source_target_pairs={{0,1},{1,2},{2,3},{4,5},{5,6},{6,7},{8,9},{9,10},{10,11},{12,13},{... | collective-permute-start | bytes 294920 | tf_op jit(solution)/shard_map/ppermute | solution.py:456
  135.7 2.1 %collective-permute-start.3 = (bf16[6,32,256]{2,1,0:T(8,128)(2,1)S(1)}, bf16[6,32,256]{2,1,0:T(8,128)(2,1)S(1)}, u32[]{:S(2)}, u32[]{:S(2)}) collective-permute-start(bf16[6,32,256]{2,1,0:T(8,128)(2,1)S(1)} %get-tuple-element.22), channel_id=1, source_target_pairs={{1,0},{2,1},{3,2},{5,4},{6,5},{7,6},{9,8},{10,9},{11,10},{13,12},{... | collective-permute-start | bytes 294920 | tf_op jit(solution)/shard_map/ppermute | solution.py:456
  137.7 13.1 %collective-permute-done.before_x.b0x = bf16[6,32,256]{2,1,0:T(8,128)(2,1)S(1)} collective-permute-done((bf16[6,32,256]{2,1,0:T(8,128)(2,1)S(1)}, bf16[6,32,256]{2,1,0:T(8,128)(2,1)S(1)}, u32[]{:S(2)}, u32[]{:S(2)}) %collective-permute-start) | collective-permute-done | bytes 98336 | tf_op jit(solution)/shard_map/ppermute | solution.py:456
  153.3 1.9 %collective-permute-start.4 = (bf16[6,32,256]{2,1,0:T(8,128)(2,1)S(1)}, bf16[6,32,256]{2,1,0:T(8,128)(2,1)S(1)}, u32[]{:S(2)}, u32[]{:S(2)}) collective-permute-start(bf16[6,32,256]{2,1,0:T(8,128)(2,1)S(1)} %get-tuple-element.29), channel_id=1, source_target_pairs={{0,4},{4,8},{8,12},{12,16},{16,20},{20,24},{24,28},{1,5},{5,9},{9,... | collective-permute-start | bytes 294920 | tf_op jit(solution)/shard_map/ppermute | solution.py:456
  155.3 4.3 %collective-permute-start.5 = (bf16[6,32,256]{2,1,0:T(8,128)(2,1)S(1)}, bf16[6,32,256]{2,1,0:T(8,128)(2,1)S(1)}, u32[]{:S(2)}, u32[]{:S(2)}) collective-permute-start(bf16[6,32,256]{2,1,0:T(8,128)(2,1)S(1)} %get-tuple-element.30), channel_id=1, source_target_pairs={{4,0},{8,4},{12,8},{16,12},{20,16},{24,20},{28,24},{5,1},{9,5},{13... | collective-permute-start | bytes 294920 | tf_op jit(solution)/shard_map/ppermute | solution.py:456
  159.5 4.0 %collective-permute-start.6 = (bf16[6,32,256]{2,1,0:T(8,128)(2,1)S(1)}, bf16[6,32,256]{2,1,0:T(8,128)(2,1)S(1)}, u32[]{:S(2)}, u32[]{:S(2)}) collective-permute-start(bf16[6,32,256]{2,1,0:T(8,128)(2,1)S(1)} %get-tuple-element.31), channel_id=1, source_target_pairs={{0,1},{1,2},{2,3},{4,5},{5,6},{6,7},{8,9},{9,10},{10,11},{12,13},{... | collective-permute-start | bytes 294920 | tf_op jit(solution)/shard_map/ppermute | solution.py:456
  163.6 2.1 %collective-permute-start.7 = (bf16[6,32,256]{2,1,0:T(8,128)(2,1)S(1)}, bf16[6,32,256]{2,1,0:T(8,128)(2,1)S(1)}, u32[]{:S(2)}, u32[]{:S(2)}) collective-permute-start(bf16[6,32,256]{2,1,0:T(8,128)(2,1)S(1)} %get-tuple-element.32), channel_id=1, source_target_pairs={{1,0},{2,1},{3,2},{5,4},{6,5},{7,6},{9,8},{10,9},{11,10},{13,12},{... | collective-permute-start | bytes 294920 | tf_op jit(solution)/shard_map/ppermute | solution.py:456
  165.7 3.8 %collective-permute-done.7.a1y = bf16[6,32,256]{2,1,0:T(8,128)(2,1)S(1)} collective-permute-done((bf16[6,32,256]{2,1,0:T(8,128)(2,1)S(1)}, bf16[6,32,256]{2,1,0:T(8,128)(2,1)S(1)}, u32[]{:S(2)}, u32[]{:S(2)}) %collective-permute-start.7) | collective-permute-done | bytes 98336 | tf_op jit(solution)/shard_map/ppermute | solution.py:456
  169.5 5.8 %shard_map.94 = f32[3,32,32,256]{3,2,1,0:T(8,128)} custom-call(bf16[32,32,256]{2,1,0:T(8,128)(2,1)S(1)} %copy-done.10, bf16[32,32,256]{2,1,0:T(8,128)(2,1)S(1)} %get-tuple-element.23.state, f32[32,32,256]{2,1,0:T(8,128)S(1)} %shard_map.90.divergence, bf16[8,32,1024]{2,1,0:T(8,128)(2,1)S(1)} %copy-done.18, bf16[8,32,1024]{2,1,0:T(8,128)(2,1)S(1)} %copy-done.20, ...), custom_call_target="tpu_custom_call" | custom-call | flops 2147483648 | bytes 8388608 | tf_op jit(solution)/shard_map/pallas_call | solution.py:539
  175.4 4.2 %shard_map.95 = bf16[32,32,256]{2,1,0:T(8,128)(2,1)} custom-call(s32[2,1,1,8]{3,2,1,0:T(1,128)S(1)} %copy-done.16, s32[2,1,1,8,1]{4,3,2,1,0:T(8,128)S(1)} %copy.19.refs_1_, bf16[64,3,32,32]{3,2,1,0:T(8,128)(2,1)S(1)} %copy-done.4, bf16[16,32,1024]{2,1,0:T(8,128)(2,1)} %all-to-all-done.3.refs_3_), custom_call_target="tpu_custom_call" | custom-call | flops 2147483648 | bytes 8388608 | tf_op jit(solution)/shard_map/pallas_call | solution.py:547
  (68 shorter events, 16.5 us)
Async XLA Ops:
  5.4 3.4 %copy-start.1 = (bf16[64,3,32,32]{3,2,1,0:T(8,128)(2,1)}, bf16[64,3,32,32]{3,2,1,0:T(8,128)(2,1)S(1)}, u32[]{:S(2)}) copy-start(bf16[64,3,32,32]{3,2,1,0:T(8,128)(2,1)S(1)} %copy.20.refs_2_.refs_3_) | copy-start | bytes 1179652
  5.4 9.5 %copy-start.24 = (s32[2,1,1,8]{3,2,1,0:T(1,128)S(1)}, s32[2,1,1,8]{3,2,1,0:T(1,128)}, u32[]{:S(2)}) copy-start(s32[2,1,1,8]{3,2,1,0:T(1,128)} %param.12) | copy-start | bytes 196
  5.4 10.3 %copy-start.23 = (s32[2,1,1,8,1]{3,4,2,1,0:T(1,128)S(1)}, s32[2,1,1,8,1]{3,4,2,1,0:T(1,128)}, u32[]{:S(2)}) copy-start(s32[2,1,1,8,1]{3,4,2,1,0:T(1,128)} %param.11) | copy-start | bytes 196
  5.4 41.0 %copy-start.16 = (s32[2,1,1,8]{3,2,1,0:T(1,128)S(1)}, s32[2,1,1,8]{3,2,1,0:T(1,128)}, u32[]{:S(2)}) copy-start(s32[2,1,1,8]{3,2,1,0:T(1,128)} %refs_0_.7) | copy-start | bytes 196
  8.8 37.6 %all-to-all-start = ((bf16[16,32,1024]{2,1,0:T(8,128)(2,1)}), bf16[16,32,1024]{2,1,0:T(8,128)(2,1)}, u32[]{:S(2)}, u32[]{:S(2)}) async-start(bf16[16,32,1024]{2,1,0:T(8,128)(2,1)} %shard_map.87), calls=%async_computation | async-start | bytes 2097152 | tf_op jit(solution)/shard_map/all_to_all | solution.py:461
  46.4 12.5 %copy-start = (f32[3,32,32,256]{3,2,1,0:T(8,128)S(1)}, f32[3,32,32,256]{3,2,1,0:T(8,128)}, u32[]{:S(2)}) copy-start(f32[3,32,32,256]{3,2,1,0:T(8,128)} %velocity.1) | copy-start | bytes 9437188
  53.7 25.7 %all-to-all-start.1 = ((bf16[16,32,1024]{2,1,0:T(8,128)(2,1)}), bf16[16,32,1024]{2,1,0:T(8,128)(2,1)}, u32[]{:S(2)}, u32[]{:S(2)}) async-start(bf16[16,32,1024]{2,1,0:T(8,128)(2,1)} %copy-done.6), calls=%async_computation.1 | async-start | bytes 2097152 | tf_op jit(solution)/shard_map/all_to_all | solution.py:461
  61.0 18.5 %copy-start.12 = (s32[2,16]{1,0:T(2,128)S(1)}, s32[2,16]{1,0:T(2,128)}, u32[]{:S(2)}) copy-start(s32[2,16]{1,0:T(2,128)} %shard_map.86.refs_2_.landing) | copy-start | bytes 388
  80.5 32.9 %copy-start.3 = (bf16[64,3,32,32]{3,2,1,0:T(8,128)(2,1)S(1)}, bf16[64,3,32,32]{3,2,1,0:T(8,128)(2,1)}, u32[]{:S(2)}) copy-start(bf16[64,3,32,32]{3,2,1,0:T(8,128)(2,1)} %copy-done.1) | copy-start | bytes 1179652
  82.7 33.7 %copy-start.17 = (bf16[8,32,1024]{2,1,0:T(8,128)(2,1)}, bf16[8,32,1024]{2,1,0:T(8,128)(2,1)S(1)}, u32[]{:S(2)}) copy-start(bf16[8,32,1024]{2,1,0:T(8,128)(2,1)S(1)} %get-tuple-element.26.adjoint_two) | copy-start | bytes 1572868
  118.1 57.2 %all-to-all-start.3 = ((bf16[16,32,1024]{2,1,0:T(8,128)(2,1)}), bf16[16,32,1024]{2,1,0:T(8,128)(2,1)}, u32[]{:S(2)}, u32[]{:S(2)}) async-start(bf16[16,32,1024]{2,1,0:T(8,128)(2,1)} %copy-done.5), calls=%async_computation.3 | async-start | bytes 2097152 | tf_op jit(solution)/shard_map/all_to_all | solution.py:461
  123.7 27.2 %collective-permute-start = (bf16[6,32,256]{2,1,0:T(8,128)(2,1)S(1)}, bf16[6,32,256]{2,1,0:T(8,128)(2,1)S(1)}, u32[]{:S(2)}, u32[]{:S(2)}) collective-permute-start(bf16[6,32,256]{2,1,0:T(8,128)(2,1)S(1)} %get-tuple-element.19), channel_id=1, source_target_pairs={{0,4},{4,8},{8,12},{12,16},{16,20},{20,24},{24,28},{1,5},{5,9},{9,... | collective-permute-start | bytes 294920 | tf_op jit(solution)/shard_map/ppermute | solution.py:456
  126.8 24.1 %collective-permute-start.1 = (bf16[6,32,256]{2,1,0:T(8,128)(2,1)S(1)}, bf16[6,32,256]{2,1,0:T(8,128)(2,1)S(1)}, u32[]{:S(2)}, u32[]{:S(2)}) collective-permute-start(bf16[6,32,256]{2,1,0:T(8,128)(2,1)S(1)} %get-tuple-element.20), channel_id=1, source_target_pairs={{4,0},{8,4},{12,8},{16,12},{20,16},{24,20},{28,24},{5,1},{9,5},{13... | collective-permute-start | bytes 294920 | tf_op jit(solution)/shard_map/ppermute | solution.py:456
  129.9 21.0 %collective-permute-start.2 = (bf16[6,32,256]{2,1,0:T(8,128)(2,1)S(1)}, bf16[6,32,256]{2,1,0:T(8,128)(2,1)S(1)}, u32[]{:S(2)}, u32[]{:S(2)}) collective-permute-start(bf16[6,32,256]{2,1,0:T(8,128)(2,1)S(1)} %get-tuple-element.21), channel_id=1, source_target_pairs={{0,1},{1,2},{2,3},{4,5},{5,6},{6,7},{8,9},{9,10},{10,11},{12,13},{... | collective-permute-start | bytes 294920 | tf_op jit(solution)/shard_map/ppermute | solution.py:456
  135.7 16.7 %copy-start.22 = (bf16[8,32,1024]{2,1,0:T(8,128)(2,1)S(1)}, bf16[8,32,1024]{2,1,0:T(8,128)(2,1)}, u32[]{:S(2)}) copy-start(bf16[8,32,1024]{2,1,0:T(8,128)(2,1)} %copy-done.21) | copy-start | bytes 1572868
  135.7 15.2 %collective-permute-start.3 = (bf16[6,32,256]{2,1,0:T(8,128)(2,1)S(1)}, bf16[6,32,256]{2,1,0:T(8,128)(2,1)S(1)}, u32[]{:S(2)}, u32[]{:S(2)}) collective-permute-start(bf16[6,32,256]{2,1,0:T(8,128)(2,1)S(1)} %get-tuple-element.22), channel_id=1, source_target_pairs={{1,0},{2,1},{3,2},{5,4},{6,5},{7,6},{9,8},{10,9},{11,10},{13,12},{... | collective-permute-start | bytes 294920 | tf_op jit(solution)/shard_map/ppermute | solution.py:456
  152.3 17.2 %copy-start.10 = (bf16[32,32,256]{2,1,0:T(8,128)(2,1)S(1)}, bf16[32,32,256]{2,1,0:T(8,128)(2,1)}, u32[]{:S(2)}) copy-start(bf16[32,32,256]{2,1,0:T(8,128)(2,1)} %template.3) | copy-start | bytes 1572868
  152.4 17.1 %copy-start.18 = (bf16[8,32,1024]{2,1,0:T(8,128)(2,1)S(1)}, bf16[8,32,1024]{2,1,0:T(8,128)(2,1)}, u32[]{:S(2)}) copy-start(bf16[8,32,1024]{2,1,0:T(8,128)(2,1)} %copy-done.17) | copy-start | bytes 1572868
  152.4 17.1 %copy-start.20 = (bf16[8,32,1024]{2,1,0:T(8,128)(2,1)S(1)}, bf16[8,32,1024]{2,1,0:T(8,128)(2,1)}, u32[]{:S(2)}) copy-start(bf16[8,32,1024]{2,1,0:T(8,128)(2,1)} %copy-done.19) | copy-start | bytes 1572868
  153.3 12.3 %collective-permute-start.4 = (bf16[6,32,256]{2,1,0:T(8,128)(2,1)S(1)}, bf16[6,32,256]{2,1,0:T(8,128)(2,1)S(1)}, u32[]{:S(2)}, u32[]{:S(2)}) collective-permute-start(bf16[6,32,256]{2,1,0:T(8,128)(2,1)S(1)} %get-tuple-element.29), channel_id=1, source_target_pairs={{0,4},{4,8},{8,12},{12,16},{16,20},{20,24},{24,28},{1,5},{5,9},{9,... | collective-permute-start | bytes 294920 | tf_op jit(solution)/shard_map/ppermute | solution.py:456
  155.3 10.4 %collective-permute-start.5 = (bf16[6,32,256]{2,1,0:T(8,128)(2,1)S(1)}, bf16[6,32,256]{2,1,0:T(8,128)(2,1)S(1)}, u32[]{:S(2)}, u32[]{:S(2)}) collective-permute-start(bf16[6,32,256]{2,1,0:T(8,128)(2,1)S(1)} %get-tuple-element.30), channel_id=1, source_target_pairs={{4,0},{8,4},{12,8},{16,12},{20,16},{24,20},{28,24},{5,1},{9,5},{13... | collective-permute-start | bytes 294920 | tf_op jit(solution)/shard_map/ppermute | solution.py:456
  159.5 6.2 %collective-permute-start.6 = (bf16[6,32,256]{2,1,0:T(8,128)(2,1)S(1)}, bf16[6,32,256]{2,1,0:T(8,128)(2,1)S(1)}, u32[]{:S(2)}, u32[]{:S(2)}) collective-permute-start(bf16[6,32,256]{2,1,0:T(8,128)(2,1)S(1)} %get-tuple-element.31), channel_id=1, source_target_pairs={{0,1},{1,2},{2,3},{4,5},{5,6},{6,7},{8,9},{9,10},{10,11},{12,13},{... | collective-permute-start | bytes 294920 | tf_op jit(solution)/shard_map/ppermute | solution.py:456
  163.6 5.9 %collective-permute-start.7 = (bf16[6,32,256]{2,1,0:T(8,128)(2,1)S(1)}, bf16[6,32,256]{2,1,0:T(8,128)(2,1)S(1)}, u32[]{:S(2)}, u32[]{:S(2)}) collective-permute-start(bf16[6,32,256]{2,1,0:T(8,128)(2,1)S(1)} %get-tuple-element.32), channel_id=1, source_target_pairs={{1,0},{2,1},{3,2},{5,4},{6,5},{7,6},{9,8},{10,9},{11,10},{13,12},{... | collective-permute-start | bytes 294920 | tf_op jit(solution)/shard_map/ppermute | solution.py:456
  169.5 5.9 %copy-start.4 = (bf16[64,3,32,32]{3,2,1,0:T(8,128)(2,1)S(1)}, bf16[64,3,32,32]{3,2,1,0:T(8,128)(2,1)}, u32[]{:S(2)}) copy-start(bf16[64,3,32,32]{3,2,1,0:T(8,128)(2,1)} %copy-done.1) | copy-start | bytes 1179652
  (12 other events, 11.4 us)
